TPU v7x, 512 devices: a whole 4x4x16 slice. The times are simulated.
512 devices in a mesh: section: 32 (over z_lo, y), tensor: 16 (over x, z_hi, core).
Axes of the slice: x: 4, y: 4, z: 16 (z_hi: 2, z_lo: 8; z = z_hi * 8 + z_lo), core: 2. Of those that a mesh axis runs over, the one named last changes fastest.
Arguments:
- grad_codes: int32 [64, 256, 12288], P('section', None, 'tensor'), may hold values from -127 to 127
- token_scales: float32 [64, 256], P('section'), may hold values from 0.003 to 0.03
- loss_grads: bfloat16 [5, 256, 12288], P(None, None, 'tensor'), may hold values from -6 to 6
- entry_order: int32 [5], replicated, may hold values from 0 to 4, each once
- w_up: bfloat16 [64, 12288, 256], P('section', 'tensor'), may hold values from -0.375 to 0.375
- w_down: bfloat16 [64, 256, 12288], P('section', None, 'tensor'), may hold values from -0.0546875 to 0.0546875
- pre_act: bfloat16 [64, 5, 256, 256], P('section'), may hold values from -6 to 6
Outputs:
- held_grads: bfloat16 [64, 256, 12288], P('section', None, 'tensor')
- down_grad: bfloat16 [64, 256, 12288], P('section', None, 'tensor')
Inputs may be any that keep to these rules, and one draw needn't show every extreme that they name: entry_order is a permutation of 0 .. 4.
All inputs are finite; a program needn't handle non-finite values.
Results may differ from a plain program's by a relative error of at most 0.015.
Values may be sent and summed in bfloat16 or wider, within the bound.
A program may use at most 64 MiB of HBM per device.

v0:
```python
import jax
import jax.numpy as jnp
from jax import lax
from jax.sharding import PartitionSpec as P

TICKS = 5


def from_behind(shard, axis, by):
    size = lax.axis_size(axis)
    return lax.ppermute(shard, axis, [(i, (i + by) % size) for i in range(size)])


def per_device(grad_codes, token_scales, loss_grads, entry_order, w_up, w_down, pre_act):
    held_rows = (grad_codes.astype(jnp.float32) * token_scales[:, :, None]).astype(jnp.bfloat16)
    weight_grad = jnp.zeros((w_down.shape[0], w_down.shape[1], w_down.shape[2]), jnp.float32)
    section_count = lax.axis_size("section")
    is_final = lax.axis_index("section") == section_count - 1
    for tick_index in range(TICKS):
        pre_tick = pre_act[:, tick_index]
        partial_value = jnp.einsum(
            "cmd,cfd->cmf", held_rows, w_down, preferred_element_type=jnp.float32
        )
        hidden = lax.psum(partial_value, "tensor")
        masked = jnp.where(pre_tick > 0, hidden, 0.0).astype(jnp.bfloat16)
        branch_term = jnp.einsum("cmf,cdf->cmd", masked, w_up, preferred_element_type=jnp.float32)
        passed = (held_rows.astype(jnp.float32) + branch_term).astype(jnp.bfloat16)
        active = jnp.maximum(pre_tick, 0)
        weight_grad = weight_grad + jnp.einsum(
            "cmf,cmd->cfd", active, held_rows, preferred_element_type=jnp.float32
        )
        entering = lax.dynamic_index_in_dim(loss_grads, entry_order[tick_index], 0, keepdims=False)
        arrived = from_behind(passed, "section", -1)
        from_low = arrived[0]
        from_high = arrived[1]
        group_low = jnp.where(is_final, from_high, from_low)
        group_high = jnp.where(is_final, entering, from_high)
        held_rows = jnp.stack([group_low, group_high], 0)
    return (held_rows, weight_grad.astype(jnp.bfloat16))


def solution(mesh):
    placed = (
        P("section", None, "tensor"),
        P("section", None),
        P(None, None, "tensor"),
        P(),
        P("section", "tensor", None),
        P("section", None, "tensor"),
        P("section", None, None, None),
    )
    return jax.shard_map(
        per_device,
        mesh=mesh,
        in_specs=placed,
        out_specs=(P("section", None, "tensor"), P("section", None, "tensor")),
        check_vma=False,
    )
```

profile of v0, /device:TPU:1, one launch (start us, length us, event | category | flops | bytes accessed | tf_op | source)
XLA Modules:
  0.0 832.5 jit_solution(2081315307371230774)
XLA Ops:
  0.6 0.0 copy-start
  0.7 2.4 fusion.60
  3.1 0.1 copy.24
  3.2 0.2 multiply_convert_fusion
  3.5 0.9 copy-done.23
  4.4 0.4 fusion.62
  4.8 141.5 %all-reduce.5 = bf16[2,256,256]{1,2,0:T(8,128)(2,1)S(1)} all-reduce(f32[2,256,256]{1,2,0:T(8,128)S(1)} %fusion.62), channel_id=1, replica_groups=mesh['section'=32,'tensor'=16] {'tensor'}, use_global_device_ids=true, to_apply=%region_0.0 | all-reduce | flops 131072 | bytes 786432 | tf_op jit(solution)/shard_map/psum | solution.py:24
  146.3 1.3 add_convert_fusion.5
  147.6 5.1 collective-permute-start
  152.7 0.7 fusion.61
  154.7 0.1 copy.25
  155.5 6.5 collective-permute-done
  162.0 1.3 slice_select_fusion.4
  163.3 1.8 fusion.26
  165.1 146.1 %all-reduce.6 = bf16[2,256,256]{1,2,0:T(8,128)(2,1)} all-reduce(f32[2,256,256]{1,2,0:T(8,128)S(1)} %fusion.26), channel_id=1, replica_groups=mesh['section'=32,'tensor'=16] {'tensor'}, use_global_device_ids=true, to_apply=%region_1.2 | all-reduce | flops 131072 | bytes 786432 | tf_op jit(solution)/shard_map/psum | solution.py:24
  311.2 2.3 add_convert_fusion.4
  313.5 6.3 collective-permute-start.1
  321.1 0.1 copy.26
  321.9 7.2 collective-permute-done.1
  329.1 1.3 slice_select_fusion.3
  330.4 1.8 fusion.25
  332.2 144.3 %all-reduce.7 = bf16[2,256,256]{1,2,0:T(8,128)(2,1)} all-reduce(f32[2,256,256]{1,2,0:T(8,128)S(1)} %fusion.25), channel_id=1, replica_groups=mesh['section'=32,'tensor'=16] {'tensor'}, use_global_device_ids=true, to_apply=%region_2.3 | all-reduce | flops 131072 | bytes 786432 | tf_op jit(solution)/shard_map/psum | solution.py:24
  476.5 2.3 add_convert_fusion.3
  478.9 6.9 collective-permute-start.2
  487.1 0.1 copy.27
  487.9 7.1 collective-permute-done.2
  495.0 1.3 slice_select_fusion.2
  496.3 2.6 fusion.24
  498.9 140.8 %all-reduce.8 = bf16[2,256,256]{1,2,0:T(8,128)(2,1)S(1)} all-reduce(f32[2,256,256]{1,2,0:T(8,128)} %fusion.24), channel_id=1, replica_groups=mesh['section'=32,'tensor'=16] {'tensor'}, use_global_device_ids=true, to_apply=%region_3.4 | all-reduce | flops 131072 | bytes 786432 | tf_op jit(solution)/shard_map/psum | solution.py:24
  639.8 1.3 add_convert_fusion.2
  641.1 11.6 %collective-permute-start.3 = (bf16[2,256,768]{2,1,0:T(8,128)(2,1)}, bf16[2,256,768]{2,1,0:T(8,128)(2,1)}, u32[]{:S(2)}, u32[]{:S(2)}) collective-permute-start(bf16[2,256,768]{2,1,0:T(8,128)(2,1)} %add_convert_fusion.2), channel_id=1, source_target_pairs={{0,496},{16,0},{32,16},{48,32},{64,48},{80,64},{96,80},{112,96},{1... | collective-permute-start | bytes 2359304 | tf_op jit(solution)/shard_map/ppermute | solution.py:11
  655.5 0.9 copy.28
  657.7 0.4 fusion.11
  658.0 2.7 fusion.9
  660.8 2.3 collective-permute-done.3
  663.0 1.3 slice_select_fusion.1
  664.3 1.2 fusion.23
  665.5 142.1 %all-reduce.9 = bf16[2,256,256]{1,2,0:T(8,128)(2,1)} all-reduce(f32[2,256,256]{1,2,0:T(8,128)} %fusion.23), channel_id=1, replica_groups=mesh['section'=32,'tensor'=16] {'tensor'}, use_global_device_ids=true, to_apply=%region_4.5 | all-reduce | flops 131072 | bytes 786432 | tf_op jit(solution)/shard_map/psum | solution.py:24
  807.6 1.5 add_convert_fusion.1
  809.2 12.4 %collective-permute-start.4 = (bf16[2,256,768]{2,1,0:T(8,128)(2,1)S(1)}, bf16[2,256,768]{2,1,0:T(8,128)(2,1)S(1)}, u32[]{:S(2)}, u32[]{:S(2)}) collective-permute-start(bf16[2,256,768]{2,1,0:T(8,128)(2,1)S(1)} %add_convert_fusion.1), channel_id=1, source_target_pairs={{0,496},{16,0},{32,16},{48,32},{64,48},{80,64},{96,80},{112,96},{1... | collective-permute-start | bytes 2359304 | tf_op jit(solution)/shard_map/ppermute | solution.py:11
  821.6 0.4 fusion.7
  822.1 0.4 fusion.5
  822.4 1.0 copy-done.1
  823.4 0.0 copy-done.21
  823.5 1.5 add_convert_fusion
  824.9 5.6 collective-permute-done.4
  830.5 1.1 slice_select_fusion
  831.6 0.9 pad_maximum_fusion.4
  (50 shorter events, 0.1 us)
Async XLA Ops:
  0.6 145.6 %copy-start = (bf16[2,768,256]{2,1,0:T(8,128)(2,1)S(1)}, bf16[2,768,256]{2,1,0:T(8,128)(2,1)}, u32[]{:S(2)}) copy-start(bf16[2,768,256]{2,1,0:T(8,128)(2,1)} %param.11) | copy-start | bytes 2359300
  0.6 2.6 copy-start.12
  0.7 2.6 copy-start.26
  3.2 1.1 copy-start.23
  146.3 6.5 copy-start.25
  146.3 8.4 %copy-start.22 = (bf16[2,1,256,256]{3,2,1,0:T(8,128)(2,1)S(1)}, bf16[2,1,256,256]{3,2,1,0:T(8,128)(2,1)}, u32[]{:S(2)}) copy-start(bf16[2,1,256,256]{3,2,1,0:T(8,128)(2,1)} %get-tuple-element.5) | copy-start | bytes 786436
  147.6 14.4 %collective-permute-start = (bf16[2,256,768]{2,1,0:T(8,128)(2,1)}, bf16[2,256,768]{2,1,0:T(8,128)(2,1)}, u32[]{:S(2)}, u32[]{:S(2)}) collective-permute-start(bf16[2,256,768]{2,1,0:T(8,128)(2,1)} %add_convert_fusion.5), channel_id=1, source_target_pairs={{0,496},{16,0},{32,16},{48,32},{64,48},{80,64},{96,80},{112,96},{1... | collective-permute-start | bytes 2359304 | tf_op jit(solution)/shard_map/ppermute | solution.py:11
  154.8 156.4 %copy-start.14 = (bf16[2,1,256,256]{2,3,0,1:T(8,128)(2,1)}, bf16[2,1,256,256]{2,3,0,1:T(8,128)(2,1)S(1)}, u32[]{:S(2)}) copy-start(bf16[2,1,256,256]{2,3,0,1:T(8,128)(2,1)S(1)} %copy.25) | copy-start | bytes 786436
  163.3 147.9 %copy-start.2 = (bf16[1,256,768]{2,1,0:T(8,128)(2,1)}, bf16[1,256,768]{2,1,0:T(8,128)(2,1)S(1)}, u32[]{:S(2)}) copy-start(bf16[1,256,768]{2,1,0:T(8,128)(2,1)S(1)} %get-tuple-element.15) | copy-start | bytes 1179652
  163.3 147.9 %copy-start.3 = (bf16[1,256,768]{2,1,0:T(8,128)(2,1)}, bf16[1,256,768]{2,1,0:T(8,128)(2,1)S(1)}, u32[]{:S(2)}) copy-start(bf16[1,256,768]{2,1,0:T(8,128)(2,1)S(1)} %get-tuple-element.16) | copy-start | bytes 1179652
  311.2 9.9 %copy-start.20 = (bf16[2,1,256,256]{3,2,1,0:T(8,128)(2,1)S(1)}, bf16[2,1,256,256]{3,2,1,0:T(8,128)(2,1)}, u32[]{:S(2)}) copy-start(bf16[2,1,256,256]{3,2,1,0:T(8,128)(2,1)} %get-tuple-element.4) | copy-start | bytes 786436
  313.5 15.6 %collective-permute-start.1 = (bf16[2,256,768]{2,1,0:T(8,128)(2,1)}, bf16[2,256,768]{2,1,0:T(8,128)(2,1)}, u32[]{:S(2)}, u32[]{:S(2)}) collective-permute-start(bf16[2,256,768]{2,1,0:T(8,128)(2,1)} %add_convert_fusion.4), channel_id=1, source_target_pairs={{0,496},{16,0},{32,16},{48,32},{64,48},{80,64},{96,80},{112,96},{1... | collective-permute-start | bytes 2359304 | tf_op jit(solution)/shard_map/ppermute | solution.py:11
  321.2 155.3 %copy-start.15 = (bf16[2,1,256,256]{2,3,0,1:T(8,128)(2,1)}, bf16[2,1,256,256]{2,3,0,1:T(8,128)(2,1)S(1)}, u32[]{:S(2)}) copy-start(bf16[2,1,256,256]{2,3,0,1:T(8,128)(2,1)S(1)} %copy.26) | copy-start | bytes 786436
  330.4 146.2 %copy-start.4 = (bf16[1,256,768]{2,1,0:T(8,128)(2,1)}, bf16[1,256,768]{2,1,0:T(8,128)(2,1)S(1)}, u32[]{:S(2)}) copy-start(bf16[1,256,768]{2,1,0:T(8,128)(2,1)S(1)} %get-tuple-element.13) | copy-start | bytes 1179652
  330.4 146.1 %copy-start.6 = (bf16[1,256,768]{2,1,0:T(8,128)(2,1)}, bf16[1,256,768]{2,1,0:T(8,128)(2,1)S(1)}, u32[]{:S(2)}) copy-start(bf16[1,256,768]{2,1,0:T(8,128)(2,1)S(1)} %get-tuple-element.14) | copy-start | bytes 1179652
  476.5 10.6 %copy-start.17 = (bf16[2,1,256,256]{3,2,1,0:T(8,128)(2,1)S(1)}, bf16[2,1,256,256]{3,2,1,0:T(8,128)(2,1)}, u32[]{:S(2)}) copy-start(bf16[2,1,256,256]{3,2,1,0:T(8,128)(2,1)} %get-tuple-element.3) | copy-start | bytes 786436
  478.9 16.1 %collective-permute-start.2 = (bf16[2,256,768]{2,1,0:T(8,128)(2,1)}, bf16[2,256,768]{2,1,0:T(8,128)(2,1)}, u32[]{:S(2)}, u32[]{:S(2)}) collective-permute-start(bf16[2,256,768]{2,1,0:T(8,128)(2,1)} %add_convert_fusion.3), channel_id=1, source_target_pairs={{0,496},{16,0},{32,16},{48,32},{64,48},{80,64},{96,80},{112,96},{1... | collective-permute-start | bytes 2359304 | tf_op jit(solution)/shard_map/ppermute | solution.py:11
  487.2 152.5 %copy-start.18 = (bf16[2,1,256,256]{2,3,0,1:T(8,128)(2,1)}, bf16[2,1,256,256]{2,3,0,1:T(8,128)(2,1)S(1)}, u32[]{:S(2)}) copy-start(bf16[2,1,256,256]{2,3,0,1:T(8,128)(2,1)S(1)} %copy.27) | copy-start | bytes 786436
  496.3 143.5 %copy-start.8 = (bf16[1,256,768]{2,1,0:T(8,128)(2,1)}, bf16[1,256,768]{2,1,0:T(8,128)(2,1)S(1)}, u32[]{:S(2)}) copy-start(bf16[1,256,768]{2,1,0:T(8,128)(2,1)S(1)} %get-tuple-element.11) | copy-start | bytes 1179652
  496.3 143.5 %copy-start.10 = (bf16[1,256,768]{2,1,0:T(8,128)(2,1)}, bf16[1,256,768]{2,1,0:T(8,128)(2,1)S(1)}, u32[]{:S(2)}) copy-start(bf16[1,256,768]{2,1,0:T(8,128)(2,1)S(1)} %get-tuple-element.12) | copy-start | bytes 1179652
  639.8 15.7 %copy-start.13 = (bf16[2,1,256,256]{3,2,1,0:T(8,128)(2,1)S(1)}, bf16[2,1,256,256]{3,2,1,0:T(8,128)(2,1)}, u32[]{:S(2)}) copy-start(bf16[2,1,256,256]{3,2,1,0:T(8,128)(2,1)} %get-tuple-element.2) | copy-start | bytes 786436
  641.1 21.9 %collective-permute-start.3 = (bf16[2,256,768]{2,1,0:T(8,128)(2,1)}, bf16[2,256,768]{2,1,0:T(8,128)(2,1)}, u32[]{:S(2)}, u32[]{:S(2)}) collective-permute-start(bf16[2,256,768]{2,1,0:T(8,128)(2,1)} %add_convert_fusion.2), channel_id=1, source_target_pairs={{0,496},{16,0},{32,16},{48,32},{64,48},{80,64},{96,80},{112,96},{1... | collective-permute-start | bytes 2359304 | tf_op jit(solution)/shard_map/ppermute | solution.py:11
  660.8 3.6 copy-start.24
  807.6 14.0 %copy-start.5 = (bf16[1,256,768]{2,1,0:T(8,128)(2,1)S(1)}, bf16[1,256,768]{2,1,0:T(8,128)(2,1)}, u32[]{:S(2)}) copy-start(bf16[1,256,768]{2,1,0:T(8,128)(2,1)} %copy-done.4) | copy-start | bytes 1179652
  807.6 14.0 %copy-start.7 = (bf16[1,256,768]{2,1,0:T(8,128)(2,1)S(1)}, bf16[1,256,768]{2,1,0:T(8,128)(2,1)}, u32[]{:S(2)}) copy-start(bf16[1,256,768]{2,1,0:T(8,128)(2,1)} %copy-done.6) | copy-start | bytes 1179652
  807.6 14.0 %copy-start.16 = (bf16[2,1,256,256]{2,3,0,1:T(8,128)(2,1)S(1)}, bf16[2,1,256,256]{2,3,0,1:T(8,128)(2,1)}, u32[]{:S(2)}) copy-start(bf16[2,1,256,256]{2,3,0,1:T(8,128)(2,1)} %copy-done.15) | copy-start | bytes 786436
  809.2 12.8 %copy-start.9 = (bf16[1,256,768]{2,1,0:T(8,128)(2,1)S(1)}, bf16[1,256,768]{2,1,0:T(8,128)(2,1)}, u32[]{:S(2)}) copy-start(bf16[1,256,768]{2,1,0:T(8,128)(2,1)} %copy-done.8) | copy-start | bytes 1179652
  809.2 12.8 %copy-start.11 = (bf16[1,256,768]{2,1,0:T(8,128)(2,1)S(1)}, bf16[1,256,768]{2,1,0:T(8,128)(2,1)}, u32[]{:S(2)}) copy-start(bf16[1,256,768]{2,1,0:T(8,128)(2,1)} %copy-done.10) | copy-start | bytes 1179652
  809.2 12.8 %copy-start.19 = (bf16[2,1,256,256]{2,3,0,1:T(8,128)(2,1)S(1)}, bf16[2,1,256,256]{2,3,0,1:T(8,128)(2,1)}, u32[]{:S(2)}) copy-start(bf16[2,1,256,256]{2,3,0,1:T(8,128)(2,1)} %copy-done.18) | copy-start | bytes 786436
  809.2 21.3 %collective-permute-start.4 = (bf16[2,256,768]{2,1,0:T(8,128)(2,1)S(1)}, bf16[2,256,768]{2,1,0:T(8,128)(2,1)S(1)}, u32[]{:S(2)}, u32[]{:S(2)}) collective-permute-start(bf16[2,256,768]{2,1,0:T(8,128)(2,1)S(1)} %add_convert_fusion.1), channel_id=1, source_target_pairs={{0,496},{16,0},{32,16},{48,32},{64,48},{80,64},{96,80},{112,96},{1... | collective-permute-start | bytes 2359304 | tf_op jit(solution)/shard_map/ppermute | solution.py:11
  822.0 1.4 copy-start.1
  822.0 1.4 copy-start.21
where the time goes:
time: 845 us; the launch traced here: 833 us
  blocking collectives  715 us (85%)
  starting transfers between devices  42.4 us (5%)
  waiting for transfers between devices  28.6 us (3%)
  matrix products  22 us (3%)
  between operations  11 us (1%)
    psum x5, blocking collectives, per_device(): hidden = lax.psum(partial_value, 'tensor')  715 us
    ppermute x5, starting transfers between devices, from_behind(): lax.ppermute(shard, axis, [(i, (i + by) % size) for i in range(size)])  42.4 us
    ppermute x5, waiting for transfers between devices, from_behind(): lax.ppermute(shard, axis, [(i, (i + by) % size) for i in range(size)])  28.6 us
  transfers between devices with their start and end apart: 5, of which 5 were waited for; matrix products, arithmetic and copies ran while one was open for 1% of the time, Pallas kernels for 0%

commit v1 on v0

v1 whole, which is shorter than its diff:
```python
import jax
import jax.numpy as jnp
from jax import lax
from jax.experimental import pallas as pl
from jax.experimental.pallas import tpu as pltpu
from jax.sharding import PartitionSpec as P

MESH = pl.DeviceIdType.MESH
F32 = jnp.float32
BF16 = jnp.bfloat16
HALVES = 2


def relay_kernel(dims, codes, scales, entry, w_up, w_down, pre_act, loss_hbm, held_out, grad_out,
                 loss_in, hbuf, passed, part, rs_in, zown, zsend, zin, masked, total, grad_vmem,
                 rs_send, rs_recv, z_send, z_recv, ag_send, ag_recv, h_send, h_recv, out_sem, loss_sem):
    sections, group, ticks, tokens, width = dims
    rows = tokens // HALVES
    piece = rows // group
    chains = 2 * HALVES
    steps = ticks * chains
    sec = lax.axis_index("section")
    ten = lax.axis_index("tensor")
    x_at = lax.div(ten, 4)
    z_at = lax.rem(lax.div(ten, 2), 2)
    core_at = lax.rem(ten, 2)
    mine = x_at * 2 + core_at

    def peer(rel):
        other = lax.rem(mine + rel, group)
        return other, (sec, lax.div(other, 2) * 4 + z_at * 2 + lax.rem(other, 2))

    z_partner = (sec, x_at * 4 + (1 - z_at) * 2 + core_at)
    below = (lax.rem(sec + sections - 1, sections), ten)
    above = (lax.rem(sec + 1, sections), ten)

    barrier = pltpu.get_barrier_semaphore()
    for rel in range(1, group):
        pl.semaphore_signal(barrier, inc=1, device_id=peer(rel)[1], device_id_type=MESH)
    for other in (z_partner, below, above):
        pl.semaphore_signal(barrier, inc=1, device_id=other, device_id_type=MESH)

    is_top = sec == sections - 1
    loss_copy = pltpu.make_async_copy(loss_hbm, loss_in, loss_sem)

    @pl.when(is_top)
    def _():
        loss_copy.start()

    total[...] = jnp.zeros_like(total)
    lanes = min(128, rows)
    for slot in range(2):
        for block in range(tokens // lanes):
            at = slice(block * lanes, (block + 1) * lanes)
            across = jnp.broadcast_to(scales[slot:slot + 1, at], (lanes, lanes)).T
            for col in range(width // lanes):
                cols = slice(col * lanes, (col + 1) * lanes)
                hbuf[0, slot, at, cols] = (codes[slot, at, cols].astype(F32) * across).astype(BF16)

    @pl.when(is_top)
    def _():
        loss_copy.wait()

    pl.semaphore_wait(barrier, group + 2)

    def where_of(step):
        tick = lax.div(step, chains)
        chain = lax.rem(step, chains)
        slot = 1 - lax.rem(chain, 2)
        half = lax.div(chain, 2)
        return tick, slot, half, pl.multiple_of(half * rows, rows)

    def h_copy(step):
        tick, slot, half, row = where_of(step)
        slot_to = slot * lax.div(sec + sections - 1, sections)
        return pltpu.make_async_remote_copy(
            src_ref=passed.at[step],
            dst_ref=hbuf.at[tick + 1, slot_to, pl.ds(row, rows)],
            send_sem=h_send.at[step],
            recv_sem=h_recv.at[tick, slot_to, half],
            device_id=below,
            device_id_type=MESH,
        )

    def arrive(tick, slot, half, row):
        enters = jnp.logical_and(is_top, slot == 1)

        @pl.when(jnp.logical_and(tick >= 1, jnp.logical_not(enters)))
        def _():
            here = hbuf.at[tick, slot, pl.ds(row, rows)]
            pltpu.make_async_copy(here, here, h_recv.at[tick - 1, slot, half]).wait()

        @pl.when(jnp.logical_and(tick >= 1, enters))
        def _():
            hbuf[tick, 1, pl.ds(row, rows), :] = loss_in[entry[lax.max(tick - 1, 0)], pl.ds(row, rows), :]

    def partial_sum(step):
        tick, slot, half, row = where_of(step)
        arrive(tick, slot, half, row)
        part[step] = lax.dot_general(
            hbuf[tick, slot, pl.ds(row, rows), :], w_down[slot], (((1,), (1,)), ((), ())),
            preferred_element_type=F32).astype(BF16)
        for rel in range(1, group):
            other, device = peer(rel)
            pltpu.make_async_remote_copy(
                src_ref=part.at[step, pl.ds(pl.multiple_of(other * piece, piece), piece)],
                dst_ref=rs_in.at[step, rel - 1],
                send_sem=rs_send.at[step],
                recv_sem=rs_recv.at[step],
                device_id=device,
                device_id_type=MESH,
            ).start()

    def wait_bytes(ref, sem):
        pltpu.make_async_copy(ref, ref, sem).wait()

    own_rows = pl.ds(pl.multiple_of(mine * piece, piece), piece)

    def reduce_group(step):
        wait_bytes(rs_in.at[step], rs_recv.at[step])
        acc = part[step, own_rows, :].astype(F32)
        for rel in range(1, group):
            acc = acc + rs_in[step, rel - 1].astype(F32)
        zown[step] = acc
        zsend[step] = acc.astype(BF16)
        z_copy(step).start()

    def z_copy(step):
        return pltpu.make_async_remote_copy(
            src_ref=zsend.at[step], dst_ref=zin.at[step], send_sem=z_send.at[step], recv_sem=z_recv.at[step],
            device_id=z_partner, device_id_type=MESH)

    def mask_and_gather(step):
        tick, slot, half, row = where_of(step)
        wait_bytes(zin.at[step], z_recv.at[step])
        hidden = zown[step] + zin[step].astype(F32)
        pre = pre_act[slot, tick, pl.ds(pl.multiple_of(row + mine * piece, piece), piece), :]
        masked[step, own_rows, :] = jnp.where(pre.astype(F32) > 0, hidden, 0.0).astype(BF16)
        for rel in range(1, group):
            _, device = peer(rel)
            pltpu.make_async_remote_copy(
                src_ref=masked.at[step, own_rows],
                dst_ref=masked.at[step, own_rows],
                send_sem=ag_send.at[step],
                recv_sem=ag_recv.at[step],
                device_id=device,
                device_id_type=MESH,
            ).start()

    def update(step):
        tick, slot, half, row = where_of(step)
        wait_bytes(rs_in.at[step], ag_recv.at[step])
        branch = lax.dot_general(
            masked[step], w_up[slot], (((1,), (1,)), ((), ())), preferred_element_type=F32)
        passed[step] = (hbuf[tick, slot, pl.ds(row, rows), :].astype(F32) + branch).astype(BF16)

        @pl.when(sec + slot > 0)
        def _():
            h_copy(step).start()

    def add_weight_grad(step):
        tick, slot, half, row = where_of(step)

        @pl.when(half == HALVES - 1)
        def _():
            active = jnp.maximum(pre_act[slot, tick], 0)
            total[slot] += lax.dot_general(
                active, hbuf[tick, slot], (((0,), (0,)), ((), ())), preferred_element_type=F32)

        @pl.when(jnp.logical_and(half == HALVES - 1, tick == ticks - 1))
        def _():
            grad_vmem[slot] = total[slot].astype(BF16)
            pltpu.make_async_copy(grad_vmem.at[slot], grad_out.at[slot], out_sem.at[slot]).start()

    def body(step, carry):
        @pl.when(step < steps)
        def _():
            partial_sum(step)

        @pl.when(step >= 1)
        def _():
            mask_and_gather(step - 1)

        @pl.when(step < steps)
        def _():
            reduce_group(step)

        @pl.when(step >= 1)
        def _():
            update(step - 1)
            add_weight_grad(step - 1)

        return carry

    lax.fori_loop(0, steps + 1, body, 0)

    for slot in (1, 0):
        for half in range(HALVES):
            row = half * rows
            arrive(ticks, slot, half, row)
        pltpu.make_async_copy(hbuf.at[ticks, slot], held_out.at[slot], out_sem.at[2 + slot]).start()

    def drain(step, carry):
        tick, slot, half, row = where_of(step)
        wait_bytes(rs_in.at[step], rs_send.at[step])
        wait_bytes(rs_in.at[step], ag_send.at[step])
        wait_bytes(zsend.at[step], z_send.at[step])

        @pl.when(sec + slot > 0)
        def _():
            wait_bytes(passed.at[step], h_send.at[step])

        return carry

    lax.fori_loop(0, steps, drain, 0)
    for slot in range(2):
        pltpu.make_async_copy(grad_vmem.at[slot], grad_out.at[slot], out_sem.at[slot]).wait()
        pltpu.make_async_copy(hbuf.at[ticks, slot], held_out.at[slot], out_sem.at[2 + slot]).wait()


def solution(mesh):
    sections, tensors = mesh.shape["section"], mesh.shape["tensor"]
    group = tensors // 2

    def per_device(grad_codes, token_scales, loss_grads, entry_order, w_up, w_down, pre_act):
        slots, tokens, width = grad_codes.shape
        ticks, hid = pre_act.shape[1], pre_act.shape[3]
        rows = tokens // HALVES
        piece = rows // group
        steps = ticks * slots * HALVES
        vmem = pl.BlockSpec(memory_space=pltpu.VMEM)
        hbm = pl.BlockSpec(memory_space=pl.ANY)
        dma = pltpu.SemaphoreType.DMA
        out = jax.ShapeDtypeStruct((slots, tokens, width), BF16)
        return pl.pallas_call(
            lambda *refs: relay_kernel((sections, group, ticks, tokens, width), *refs),
            out_shape=(out, jax.ShapeDtypeStruct((slots, hid, width), BF16)),
            in_specs=[vmem, vmem, pl.BlockSpec(memory_space=pltpu.SMEM), vmem, vmem, vmem, hbm],
            out_specs=(hbm, hbm),
            scratch_shapes=[
                pltpu.VMEM((ticks, tokens, width), BF16),
                pltpu.VMEM((ticks + 1, slots, tokens, width), BF16),
                pltpu.VMEM((steps, rows, width), BF16),
                pltpu.VMEM((steps, rows, hid), BF16),
                pltpu.VMEM((steps, group - 1, piece, hid), BF16),
                pltpu.VMEM((steps, piece, hid), F32),
                pltpu.VMEM((steps, piece, hid), BF16),
                pltpu.VMEM((steps, piece, hid), BF16),
                pltpu.VMEM((steps, rows, hid), BF16),
                pltpu.VMEM((slots, hid, width), F32),
                pltpu.VMEM((slots, hid, width), BF16),
                dma((steps,)), dma((steps,)), dma((steps,)), dma((steps,)),
                dma((steps,)), dma((steps,)), dma((steps,)), dma((ticks, slots, HALVES)),
                dma((4,)), dma,
            ],
            compiler_params=pltpu.CompilerParams(
                collective_id=0, has_side_effects=True, vmem_limit_bytes=48 * 1024 * 1024),
            cost_estimate=pl.CostEstimate(flops=3 * 10**9, bytes_accessed=8 * 10**6, transcendentals=0),
        )(grad_codes, token_scales, entry_order, w_up, w_down, pre_act, loss_grads)

    placed = (
        P("section", None, "tensor"),
        P("section", None),
        P(None, None, "tensor"),
        P(),
        P("section", "tensor", None),
        P("section", None, "tensor"),
        P("section", None, None, None),
    )
    return jax.shard_map(
        per_device,
        mesh=mesh,
        in_specs=placed,
        out_specs=(P("section", None, "tensor"), P("section", None, "tensor")),
        check_vma=False,
    )
```

time: 845 us -> 194 us (0.23); the launches traced: 833 us -> 191 us
  blocking collectives: 715 us -> 0 us
  Pallas kernels: 0 us -> 182 us
  starting transfers between devices: 42.4 us -> 0 us
  waiting for transfers between devices: 28.6 us -> 0 us
  matrix products: 22 us -> 0 us
  between operations: 11 us -> 0.65 us
    psum x5 -> x0, blocking collectives: 715 us -> none  [per_device(): hidden = lax.psum(partial_value, 'tensor')]
    pallas_call x0 -> x1, Pallas kernels: none -> 182 us  [per_device(): pl.pallas_call(lambda *refs: relay_kernel((sections, group, ticks, tokens...]
    ppermute x5 -> x0, starting transfers between devices: 42.4 us -> none  [from_behind(): lax.ppermute(shard, axis, [(i, (i + by) % size) for i in range(size)])]
    ppermute x5 -> x0, waiting for transfers between devices: 28.6 us -> none  [from_behind(): lax.ppermute(shard, axis, [(i, (i + by) % size) for i in range(size)])]
    dot_general x15 -> x0, matrix products: 22 us -> none  [the longest x5 8.79 us: per_device(): jnp.einsum('cmf,cdf->cmd', masked, w_up, preferred_element_type=jnp.float32)]
  transfers between devices with their start and end apart: 5 -> 0, of which waited for: 5 -> 0; matrix products, arithmetic and copies ran while one was open for 1% -> 0% of each run, Pallas kernels for 0% -> 0%
where the time goes in v1:
time: 194 us; the launch traced here: 191 us
  Pallas kernels  182 us (94%)
  local copies, waits for them, and re-layouts  8.08 us (4%)
    pallas_call x1, Pallas kernels, per_device(): pl.pallas_call(lambda *refs: relay_kernel((sections, group, ticks, tokens...  182 us
    unnamed x14, local copies, waits for them, and re-layouts  8.08 us

profile of v1, /device:TPU:1, one launch (start us, length us, event | category | flops | bytes accessed | tf_op | source)
XLA Modules:
  0.0 190.6 jit_solution(4702381556707107638)
XLA Ops:
  0.6 0.0 copy-start
  0.6 1.4 copy-done
  2.0 0.0 copy-start.1
  2.0 1.3 copy-done.1
  3.4 0.0 copy-start.2
  3.4 1.1 copy-done.2
  4.5 0.0 copy-start.3
  4.5 1.1 copy-done.3
  5.6 0.0 copy-start.4
  5.6 0.7 copy-done.4
  6.3 0.0 copy-start.5
  6.3 0.7 copy-done.5
  7.0 181.9 %shard_map.86 = (bf16[2,256,768]{2,1,0:T(8,128)(2,1)S(1)}, bf16[2,256,768]{2,1,0:T(8,128)(2,1)S(1)}) custom-call(s32[2,256,768]{2,1,0:T(8,128)S(1)} %copy-done, f32[2,256]{1,0:T(2,128)S(1)} %copy-done.4, s32[5]{0:T(128)S(1)} %copy-done.5, bf16[2,768,256]{2,1,0:T(8,128)(2,1)S(1)} %copy-done.2, bf16[2,256,768]{2,1,0:T(8,128)(2,1)S(1)} %copy-done.3, ...), custom_call_target="tpu_custom_call" | custom-call | flops 3000000000 | bytes 8000000 | tf_op jit(solution)/shard_map/pallas_call | solution.py:235
  188.8 0.9 copy.11
  189.7 0.9 copy.12
Async XLA Ops:
  0.6 1.4 copy-start
  2.0 1.3 copy-start.1
  3.4 1.1 copy-start.2
  4.5 1.1 copy-start.3
  5.6 0.7 copy-start.4
  6.3 0.7 copy-start.5

commit v2 on v0

v2 whole, which is shorter than its diff:
```python
import jax
import jax.numpy as jnp
from jax import lax
from jax.experimental import pallas as pl
from jax.experimental.pallas import tpu as pltpu
from jax.sharding import PartitionSpec as P

MESH = pl.DeviceIdType.MESH
F32 = jnp.float32
BF16 = jnp.bfloat16
CHAINS = 4
NT = (((1,), (1,)), ((), ()))
TN = (((0,), (0,)), ((), ()))


def relay_kernel(dims, scales, entry, codes_hbm, up_hbm, down_hbm, pre_hbm, loss_hbm, held_out, grad_out,
                 codes, w_up, w_down, pre_act, loss_in, down_in, hbuf, passed, part, rs_in, gsum, msg, masked,
                 cross, total, grad_vmem, load_sem, rs_send, rs_recv, msg_send, msg_recv, ag_send, ag_recv,
                 g_send, g_recv, h_send, h_recv, down_send, down_recv, held_sem, grad_sem):
    sections, group, ticks, tokens, width = dims
    rows = tokens // 2
    piece = rows // group
    first_q, first_g, first_top = CHAINS, CHAINS * ticks, CHAINS * (ticks + 1)
    jobs_q = CHAINS * (ticks - 1)
    steps = CHAINS * ticks
    sec = lax.axis_index("section")
    ten = lax.axis_index("tensor")
    x_at = lax.div(ten, 4)
    z_at = lax.rem(lax.div(ten, 2), 2)
    core_at = lax.rem(ten, 2)
    mine = x_at * 2 + core_at
    partner = x_at * 4 + (1 - z_at) * 2 + core_at
    sec_below = lax.rem(sec + sections - 1, sections)
    sec_above = lax.rem(sec + 1, sections)
    is_top = sec == sections - 1
    keeps = lax.div(sec + sections - 1, sections)
    own_rows = pl.ds(pl.multiple_of(mine * piece, piece), piece)

    def peer(rel):
        other = lax.rem(mine + rel, group)
        return other, (sec, lax.div(other, 2) * 4 + z_at * 2 + lax.rem(other, 2))

    def send(src, dst, ssem, rsem, device):
        return pltpu.make_async_remote_copy(
            src_ref=src, dst_ref=dst, send_sem=ssem, recv_sem=rsem, device_id=device, device_id_type=MESH)

    def wait_bytes(ref, sem):
        pltpu.make_async_copy(ref, ref, sem).wait()

    barrier = pltpu.get_barrier_semaphore()
    greeted = [peer(rel)[1] for rel in range(1, group)]
    greeted += [(sec, partner), (sec_below, ten), (sec_above, ten), (sec_below, partner), (sec_above, partner)]
    for other in greeted:
        pl.semaphore_signal(barrier, inc=1, device_id=other, device_id_type=MESH)

    loads = [pltpu.make_async_copy(src, dst, load_sem.at[i]) for i, (src, dst) in enumerate((
        (codes_hbm, codes), (down_hbm, w_down), (up_hbm, w_up), (pre_hbm, pre_act), (loss_hbm, loss_in)))]
    for load in loads[:4]:
        load.start()

    @pl.when(is_top)
    def _():
        loads[4].start()

    total[...] = jnp.zeros_like(total)
    loads[0].wait()
    lanes = min(128, rows)
    for slot in range(2):
        for block in range(tokens // lanes):
            at = slice(block * lanes, (block + 1) * lanes)
            across = jnp.broadcast_to(scales[slot:slot + 1, at], (lanes, lanes)).T
            for col in range(width // lanes):
                cols = slice(col * lanes, (col + 1) * lanes)
                hbuf[0, slot, at, cols] = (codes[slot, at, cols].astype(F32) * across).astype(BF16)
    loads[1].wait()
    pl.semaphore_wait(barrier, len(greeted))

    def down_copy(slot, slot_to):
        return send(w_down.at[slot], down_in.at[slot_to], down_send.at[slot], down_recv.at[slot_to], (sec_above, ten))

    @pl.when(is_top)
    def _():
        down_copy(0, 1).start()

    @pl.when(jnp.logical_not(is_top))
    def _():
        down_copy(1, 1).start()
        down_copy(0, 0).start()

    def where_of(step):
        tick = lax.div(step, CHAINS)
        chain = lax.rem(step, CHAINS)
        half = lax.rem(chain, 2)
        return tick, 1 - lax.div(chain, 2), half, pl.multiple_of(half * rows, rows)

    def goes_down(slot):
        return sec + slot > 0

    def enters(slot):
        return sec + slot == sections

    def scatter(job):
        for rel in range(1, group):
            other, device = peer(rel)
            send(part.at[job, pl.ds(pl.multiple_of(other * piece, piece), piece)], rs_in.at[job, rel - 1],
                 rs_send.at[job], rs_recv.at[job], device).start()

    def gathered(job):
        wait_bytes(rs_in.at[job], rs_recv.at[job])
        acc = part[job, own_rows, :].astype(F32)
        for rel in range(1, group):
            acc = acc + rs_in[job, rel - 1].astype(F32)
        return acc

    def own_partial(tick, slot, row, job):
        part[job] = lax.dot_general(
            hbuf[tick, slot, pl.ds(row, rows), :], w_down[slot], NT, preferred_element_type=F32).astype(BF16)
        scatter(job)

    def own_exchange(tick, slot, half, job):
        gsum[job] = gathered(job).astype(BF16)
        msg[tick, slot, half, z_at] = gsum[job]
        send(gsum.at[job], msg.at[tick, slot, half, z_at], msg_send.at[job], msg_recv.at[tick, slot, half],
             (sec, partner)).start()

    def arrive(tick, slot, half, row):
        @pl.when(jnp.logical_not(enters(slot)))
        def _():
            wait_bytes(hbuf.at[tick, slot, pl.ds(row, rows)], h_recv.at[tick - 1, slot, half])

    def look_ahead(step):
        tick, slot, half, row = where_of(step)

        @pl.when(jnp.logical_and(step < jobs_q, goes_down(slot)))
        def _():
            job = first_q + step
            part[job] = lax.dot_general(
                hbuf[tick, slot, pl.ds(row, rows), :], down_in[slot], NT, preferred_element_type=F32).astype(BF16)
            scatter(job)

    def pass_sum(step):
        tick, slot, half, row = where_of(step)

        @pl.when(jnp.logical_and(step < jobs_q, goes_down(slot)))
        def _():
            job = first_q + step
            gsum[job] = (gathered(job) + jnp.dot(
                masked[step, own_rows, :], cross[slot], preferred_element_type=F32)).astype(BF16)
            for to in (ten, partner):
                send(gsum.at[job], msg.at[tick + 1, slot * keeps, half, z_at], msg_send.at[job],
                     msg_recv.at[tick + 1, slot * keeps, half], (sec_below, to)).start()

    def finish_hidden(step):
        tick, slot, half, row = where_of(step)
        from_own = jnp.logical_or(tick == 0, enters(slot))

        @pl.when(from_own)
        def _():
            wait_bytes(gsum.at[0], msg_recv.at[tick, slot, half])

        @pl.when(jnp.logical_not(from_own))
        def _():
            wait_bytes(msg.at[tick, slot, half], msg_recv.at[tick, slot, half])

        hidden = msg[tick, slot, half, 0].astype(F32) + msg[tick, slot, half, 1].astype(F32)
        pre = pre_act[slot, tick, pl.ds(pl.multiple_of(row + mine * piece, piece), piece), :]
        masked[step, own_rows, :] = jnp.where(pre.astype(F32) > 0, hidden, 0.0).astype(BF16)
        for rel in range(1, group):
            send(masked.at[step, own_rows], masked.at[step, own_rows], ag_send.at[step], ag_recv.at[step],
                 peer(rel)[1]).start()

    def update(step):
        tick, slot, half, row = where_of(step)
        wait_bytes(rs_in.at[0], ag_recv.at[step])

        @pl.when(goes_down(slot))
        def _():
            branch = lax.dot_general(masked[step], w_up[slot], NT, preferred_element_type=F32)
            passed[step] = (hbuf[tick, slot, pl.ds(row, rows), :].astype(F32) + branch).astype(BF16)
            send(passed.at[step], hbuf.at[tick + 1, slot * keeps, pl.ds(row, rows)], h_send.at[step],
                 h_recv.at[tick, slot * keeps, half], (sec_below, ten)).start()

    def add_weight_grad(step):
        tick, slot, half, row = where_of(step)

        @pl.when(half == 1)
        def _():
            active = jnp.maximum(pre_act[slot, tick], 0)
            total[slot] += lax.dot_general(active, hbuf[tick, slot], TN, preferred_element_type=F32)

        @pl.when(jnp.logical_and(half == 1, tick == ticks - 1))
        def _():
            grad_vmem[slot] = total[slot].astype(BF16)
            pltpu.make_async_copy(grad_vmem.at[slot], grad_out.at[slot], grad_sem.at[slot]).start()

    def cross_scatter(slot):
        @pl.when(goes_down(slot))
        def _():
            wait_bytes(down_in.at[slot], down_recv.at[slot])
            term = lax.dot_general(w_up[slot], down_in[slot], (((0,), (1,)), ((), ())), preferred_element_type=F32)
            for half in range(2):
                part[first_g + slot * 2 + half] = term[half * rows:(half + 1) * rows].astype(BF16)
                scatter(first_g + slot * 2 + half)

    def cross_gather(slot):
        @pl.when(goes_down(slot))
        def _():
            for half in range(2):
                job = first_g + slot * 2 + half
                at = pl.ds(pl.multiple_of(half * rows + mine * piece, piece), piece)
                cross[slot, at, :] = gathered(job).astype(BF16)
                for rel in range(1, group):
                    send(cross.at[slot, at], cross.at[slot, at], g_send.at[slot * 2 + half],
                         g_recv.at[slot * 2 + half], peer(rel)[1]).start()

    def cross_wait(slot):
        @pl.when(goes_down(slot))
        def _():
            for half in range(2):
                wait_bytes(rs_in.at[0], g_recv.at[slot * 2 + half])

    def each(first, last, do):
        def body(step, carry):
            do(step)
            return carry

        lax.fori_loop(first, last, body, 0)

    def start_own(step):
        tick, slot, half, row = where_of(step)
        own_partial(0, slot, row, step)

    def exchange_own(step):
        tick, slot, half, row = where_of(step)
        own_exchange(0, slot, half, step)

    each(0, CHAINS, start_own)
    loads[2].wait()
    loads[3].wait()
    each(0, CHAINS, exchange_own)

    @pl.when(is_top)
    def _():
        loads[4].wait()
        for tick in range(1, ticks + 1):
            hbuf[tick, 1] = loss_in[entry[tick - 1]]

        def start_top(job):
            half = lax.rem(job, 2)
            own_partial(1 + lax.div(job, 2), 1, pl.multiple_of(half * rows, rows), first_top + job)

        def exchange_top(job):
            own_exchange(1 + lax.div(job, 2), 1, lax.rem(job, 2), first_top + job)

        each(0, 2 * (ticks - 1), start_top)
        each(0, 2 * (ticks - 1), exchange_top)

    cross_scatter(1)
    each(0, 2, look_ahead)
    each(0, CHAINS, finish_hidden)
    cross_gather(1)
    each(0, CHAINS, update)
    cross_scatter(0)
    each(2, CHAINS, look_ahead)
    cross_wait(1)
    each(0, 2, pass_sum)
    each(0, CHAINS, add_weight_grad)
    cross_gather(0)

    def take(step):
        tick, slot, half, row = where_of(step)
        arrive(tick, slot, half, row)
        look_ahead(step)

    take(CHAINS)
    cross_wait(0)
    pass_sum(2)
    finish_hidden(CHAINS)

    def main(step):
        pass_sum(step - 1)

        @pl.when(step + 1 < steps)
        def _():
            finish_hidden(step + 1)

        update(step)

        @pl.when(step + 1 < steps)
        def _():
            take(step + 1)
            add_weight_grad(step + 1)

    each(CHAINS, steps, main)

    def held_copy(chain):
        tick, slot, half, row = where_of(chain)
        return pltpu.make_async_copy(
            hbuf.at[ticks, slot, pl.ds(row, rows)], held_out.at[slot, pl.ds(row, rows)], held_sem.at[chain])

    def hand_out(chain):
        tick, slot, half, row = where_of(chain)
        arrive(ticks, slot, half, row)
        held_copy(chain).start()

    each(0, CHAINS, hand_out)

    def drain(step):
        tick, slot, half, row = where_of(step)
        wait_bytes(rs_in.at[0], ag_send.at[step])

        @pl.when(goes_down(slot))
        def _():
            wait_bytes(passed.at[step], h_send.at[step])

        @pl.when(jnp.logical_and(step < jobs_q, goes_down(slot)))
        def _():
            wait_bytes(rs_in.at[0], rs_send.at[first_q + step])
            wait_bytes(msg.at[0, 0, 0], msg_send.at[first_q + step])

    def drain_own(job):
        wait_bytes(rs_in.at[0], rs_send.at[job])
        wait_bytes(gsum.at[0], msg_send.at[job])

    def drain_cross(job):
        @pl.when(goes_down(lax.div(job, 2)))
        def _():
            wait_bytes(rs_in.at[0], rs_send.at[first_g + job])
            wait_bytes(rs_in.at[0], g_send.at[job])

    each(0, steps, drain)
    each(0, CHAINS, drain_own)
    each(0, CHAINS, drain_cross)
    wait_bytes(w_down.at[0], down_send.at[0])

    @pl.when(is_top)
    def _():
        each(first_top, first_top + 2 * (ticks - 1), drain_own)

    @pl.when(jnp.logical_not(is_top))
    def _():
        wait_bytes(w_down.at[1], down_send.at[1])

    for slot in range(2):
        pltpu.make_async_copy(grad_vmem.at[slot], grad_out.at[slot], grad_sem.at[slot]).wait()
    for chain in range(CHAINS):
        held_copy(chain).wait()


def solution(mesh):
    sections, tensors = mesh.shape["section"], mesh.shape["tensor"]
    group = tensors // 2

    def per_device(grad_codes, token_scales, loss_grads, entry_order, w_up, w_down, pre_act):
        slots, tokens, width = grad_codes.shape
        ticks, hid = pre_act.shape[1], pre_act.shape[3]
        rows = tokens // 2
        piece = rows // group
        steps = ticks * CHAINS
        jobs = CHAINS * (ticks + 1) + 2 * (ticks - 1)
        vmem = pl.BlockSpec(memory_space=pltpu.VMEM)
        hbm = pl.BlockSpec(memory_space=pl.ANY)
        dma = pltpu.SemaphoreType.DMA
        return pl.pallas_call(
            lambda *refs: relay_kernel((sections, group, ticks, tokens, width), *refs),
            out_shape=(jax.ShapeDtypeStruct((slots, tokens, width), BF16),
                       jax.ShapeDtypeStruct((slots, hid, width), BF16)),
            in_specs=[vmem, pl.BlockSpec(memory_space=pltpu.SMEM), hbm, hbm, hbm, hbm, hbm],
            out_specs=(hbm, hbm),
            scratch_shapes=[
                pltpu.VMEM((slots, tokens, width), jnp.int32),
                pltpu.VMEM((slots, width, hid), BF16),
                pltpu.VMEM((slots, hid, width), BF16),
                pltpu.VMEM((slots, ticks, tokens, hid), BF16),
                pltpu.VMEM((ticks, tokens, width), BF16),
                pltpu.VMEM((slots, hid, width), BF16),
                pltpu.VMEM((ticks + 1, slots, tokens, width), BF16),
                pltpu.VMEM((steps, rows, width), BF16),
                pltpu.VMEM((jobs, rows, hid), BF16),
                pltpu.VMEM((jobs, group - 1, piece, hid), BF16),
                pltpu.VMEM((jobs, piece, hid), BF16),
                pltpu.VMEM((ticks, slots, 2, 2, piece, hid), BF16),
                pltpu.VMEM((steps, rows, hid), BF16),
                pltpu.VMEM((slots, hid, hid), BF16),
                pltpu.VMEM((slots, hid, width), F32),
                pltpu.VMEM((slots, hid, width), BF16),
                dma((5,)), dma((jobs,)), dma((jobs,)), dma((jobs,)), dma((ticks, slots, 2)), dma((steps,)),
                dma((steps,)), dma((CHAINS,)), dma((CHAINS,)), dma((steps,)), dma((ticks, slots, 2)),
                dma((slots,)), dma((slots,)), dma((CHAINS,)), dma((slots,)),
            ],
            compiler_params=pltpu.CompilerParams(
                collective_id=0, has_side_effects=True, vmem_limit_bytes=56 * 1024 * 1024),
            cost_estimate=pl.CostEstimate(flops=4 * 10**9, bytes_accessed=9 * 10**6, transcendentals=0),
        )(token_scales, entry_order, grad_codes, w_up, w_down, pre_act, loss_grads)

    placed = (
        P("section", None, "tensor"),
        P("section", None),
        P(None, None, "tensor"),
        P(),
        P("section", "tensor", None),
        P("section", None, "tensor"),
        P("section", None, None, None),
    )
    return jax.shard_map(
        per_device,
        mesh=mesh,
        in_specs=placed,
        out_specs=(P("section", None, "tensor"), P("section", None, "tensor")),
        check_vma=False,
    )
```

time: 845 us -> 146 us (0.17); the launches traced: 833 us -> 146 us
  blocking collectives: 715 us -> 0 us
  Pallas kernels: 0 us -> 142 us
  starting transfers between devices: 42.4 us -> 0 us
  waiting for transfers between devices: 28.6 us -> 0 us
  matrix products: 22 us -> 0 us
  between operations: 11 us -> 0.65 us
    psum x5 -> x0, blocking collectives: 715 us -> none  [per_device(): hidden = lax.psum(partial_value, 'tensor')]
    pallas_call x0 -> x1, Pallas kernels: none -> 142 us  [per_device(): pl.pallas_call(lambda *refs: relay_kernel((sections, group, ticks, tokens...]
    ppermute x5 -> x0, starting transfers between devices: 42.4 us -> none  [from_behind(): lax.ppermute(shard, axis, [(i, (i + by) % size) for i in range(size)])]
    ppermute x5 -> x0, waiting for transfers between devices: 28.6 us -> none  [from_behind(): lax.ppermute(shard, axis, [(i, (i + by) % size) for i in range(size)])]
    dot_general x15 -> x0, matrix products: 22 us -> none  [the longest x5 8.79 us: per_device(): jnp.einsum('cmf,cdf->cmd', masked, w_up, preferred_element_type=jnp.float32)]
  transfers between devices with their start and end apart: 5 -> 0, of which waited for: 5 -> 0; matrix products, arithmetic and copies ran while one was open for 1% -> 0% of each run, Pallas kernels for 0% -> 0%
where the time goes in v2:
time: 146 us
  Pallas kernels  142 us (97%)
  local copies, waits for them, and re-layouts  3.02 us (2%)
    pallas_call x1, Pallas kernels, per_device(): pl.pallas_call(lambda *refs: relay_kernel((sections, group, ticks, tokens...  142 us
    unnamed x4, local copies, waits for them, and re-layouts  3.02 us

profile of v2, /device:TPU:1, one launch (start us, length us, event | category | flops | bytes accessed | tf_op | source)
XLA Modules:
  0.0 146.0 jit_solution(7212714030821411817)
XLA Ops:
  0.6 142.4 %shard_map.86 = (bf16[2,256,768]{2,1,0:T(8,128)(2,1)}, bf16[2,256,768]{2,1,0:T(8,128)(2,1)}) custom-call(f32[2,256]{1,0:T(2,128)} %refs_0_.1, s32[5]{0:T(128)} %refs_1_.1, s32[2,256,768]{2,1,0:T(8,128)} %refs_2_.1, bf16[2,768,256]{2,1,0:T(8,128)(2,1)} %refs_3_.1, bf16[2,256,768]{2,1,0:T(8,128)(2,1)} %refs_4_.1, bf16[2,5,256,256]{3,2,1,0:T(8,128)(2,1)} %refs_5_.1, ...), custom_call_target="tpu_custom_call" | custom-call | flops 4000000000 | bytes 9000000 | tf_op jit(solution)/shard_map/pallas_call | solution.py:364
  143.0 0.0 copy-start
  143.0 2.1 %copy.11 = bf16[2,256,768]{2,1,0:T(8,128)(2,1)} copy(bf16[2,256,768]{2,1,0:T(8,128)(2,1)} %get-tuple-element.4) | data formatting | bytes 1572864
  145.2 0.0 copy-done
  145.2 0.9 copy.12
Async XLA Ops:
  143.0 2.1 %copy-start = (bf16[2,256,768]{2,1,0:T(8,128)(2,1)S(1)}, bf16[2,256,768]{2,1,0:T(8,128)(2,1)}, u32[]{:S(2)}) copy-start(bf16[2,256,768]{2,1,0:T(8,128)(2,1)} %get-tuple-element.5) | copy-start | bytes 2359300

commit v3 on v2

v3 whole, which is shorter than its diff:
```python
import jax
import jax.numpy as jnp
from jax import lax
from jax.experimental import pallas as pl
from jax.experimental.pallas import tpu as pltpu
from jax.sharding import PartitionSpec as P

MESH = pl.DeviceIdType.MESH
F32 = jnp.float32
BF16 = jnp.bfloat16
CHAINS = 4
NT = (((1,), (1,)), ((), ()))
TN = (((0,), (0,)), ((), ()))


def relay_kernel(dims, scales, entry, codes_hbm, up_hbm, down_hbm, pre_hbm, loss_hbm, held_out, grad_out,
                 codes, w_up, w_down, pre_act, loss_in, down_in, hbuf, passed, part, rs_in, gsum, msg, masked,
                 cross, total, load_sem, rs_send, rs_recv, msg_send, msg_recv, ag_send, ag_recv,
                 g_send, g_recv, h_send, h_recv, down_send, down_recv):
    sections, group, ticks, tokens, width = dims
    rows = tokens // 2
    piece = rows // group
    first_q, first_g, first_top = CHAINS, CHAINS * ticks, CHAINS * (ticks + 1)
    jobs_q = CHAINS * (ticks - 1)
    steps = CHAINS * ticks
    sec = lax.axis_index("section")
    ten = lax.axis_index("tensor")
    x_at = lax.div(ten, 4)
    z_at = lax.rem(lax.div(ten, 2), 2)
    core_at = lax.rem(ten, 2)
    mine = x_at * 2 + core_at
    partner = x_at * 4 + (1 - z_at) * 2 + core_at
    sec_below = lax.rem(sec + sections - 1, sections)
    sec_above = lax.rem(sec + 1, sections)
    is_top = sec == sections - 1
    keeps = lax.div(sec + sections - 1, sections)
    own_rows = pl.ds(pl.multiple_of(mine * piece, piece), piece)

    def peer(rel):
        other = lax.rem(mine + rel, group)
        return other, (sec, lax.div(other, 2) * 4 + z_at * 2 + lax.rem(other, 2))

    def send(src, dst, ssem, rsem, device):
        return pltpu.make_async_remote_copy(
            src_ref=src, dst_ref=dst, send_sem=ssem, recv_sem=rsem, device_id=device, device_id_type=MESH)

    def wait_bytes(ref, sem):
        pltpu.make_async_copy(ref, ref, sem).wait()

    def down_copy(slot, slot_to):
        return send(w_down.at[slot], down_in.at[slot_to], down_send.at[slot], down_recv.at[slot_to], (sec_above, ten))

    def where_of(step):
        tick = lax.div(step, CHAINS)
        chain = lax.rem(step, CHAINS)
        half = lax.rem(chain, 2)
        return tick, 1 - lax.div(chain, 2), half, pl.multiple_of(half * rows, rows)

    def goes_down(slot):
        return sec + slot > 0

    def enters(slot):
        return sec + slot == sections

    def scatter(job):
        for rel in range(1, group):
            other, device = peer(rel)
            send(part.at[job, pl.ds(pl.multiple_of(other * piece, piece), piece)], rs_in.at[job, rel - 1],
                 rs_send.at[job], rs_recv.at[job], device).start()

    def gathered(job):
        wait_bytes(rs_in.at[job], rs_recv.at[job])
        acc = part[job, own_rows, :].astype(F32)
        for rel in range(1, group):
            acc = acc + rs_in[job, rel - 1].astype(F32)
        return acc

    def own_partial(tick, slot, row, job):
        part[job] = lax.dot_general(
            hbuf[tick, slot, pl.ds(row, rows), :], w_down[slot], NT, preferred_element_type=F32).astype(BF16)
        scatter(job)

    def own_exchange(tick, slot, half, job):
        gsum[job] = gathered(job).astype(BF16)
        msg[tick, slot, half, z_at] = gsum[job]
        send(gsum.at[job], msg.at[tick, slot, half, z_at], msg_send.at[job], msg_recv.at[tick, slot, half],
             (sec, partner)).start()

    def arrive(tick, slot, half, row):
        @pl.when(jnp.logical_not(enters(slot)))
        def _():
            wait_bytes(hbuf.at[tick, slot, pl.ds(row, rows)], h_recv.at[tick - 1, slot, half])

    def look_ahead(step):
        tick, slot, half, row = where_of(step)

        @pl.when(jnp.logical_and(step < jobs_q, goes_down(slot)))
        def _():
            job = first_q + step
            part[job] = lax.dot_general(
                hbuf[tick, slot, pl.ds(row, rows), :], down_in[slot], NT, preferred_element_type=F32).astype(BF16)
            scatter(job)

    def send_sum(step):
        tick, slot, half, row = where_of(step)
        for to in (ten, partner):
            send(gsum.at[first_q + step], msg.at[tick + 1, slot * keeps, half, z_at], msg_send.at[first_q + step],
                 msg_recv.at[tick + 1, slot * keeps, half], (sec_below, to)).start()

    def pass_sum(step):
        tick, slot, half, row = where_of(step)

        @pl.when(jnp.logical_and(step < jobs_q, goes_down(slot)))
        def _():
            @pl.when(jnp.logical_and(tick == 1, half == 0))
            def _():
                for part_of in range(2):
                    wait_bytes(rs_in.at[0], g_recv.at[slot * 2 + part_of])

            gsum[first_q + step] = (gathered(first_q + step) + jnp.dot(
                masked[step, own_rows, :], cross[slot], preferred_element_type=F32)).astype(BF16)
            send_sum(step)

    def finish_hidden(step):
        tick, slot, half, row = where_of(step)
        from_own = jnp.logical_or(tick == 0, enters(slot))

        @pl.when(from_own)
        def _():
            wait_bytes(gsum.at[0], msg_recv.at[tick, slot, half])

        @pl.when(jnp.logical_not(from_own))
        def _():
            wait_bytes(msg.at[tick, slot, half], msg_recv.at[tick, slot, half])

        hidden = msg[tick, slot, half, 0].astype(F32) + msg[tick, slot, half, 1].astype(F32)
        pre = pre_act[slot, tick, pl.ds(pl.multiple_of(row + mine * piece, piece), piece), :]
        masked[step, own_rows, :] = jnp.where(pre.astype(F32) > 0, hidden, 0.0).astype(BF16)
        for rel in range(1, group):
            send(masked.at[step, own_rows], masked.at[step, own_rows], ag_send.at[step], ag_recv.at[step],
                 peer(rel)[1]).start()

    def update(step):
        tick, slot, half, row = where_of(step)
        wait_bytes(rs_in.at[0], ag_recv.at[step])

        @pl.when(goes_down(slot))
        def _():
            branch = lax.dot_general(masked[step], w_up[slot], NT, preferred_element_type=F32)
            passed[step] = (hbuf[tick, slot, pl.ds(row, rows), :].astype(F32) + branch).astype(BF16)
            send(passed.at[step], hbuf.at[tick + 1, slot * keeps, pl.ds(row, rows)], h_send.at[step],
                 h_recv.at[tick, slot * keeps, half], (sec_below, ten)).start()

    def add_weight_grad(step):
        tick, slot, half, row = where_of(step)

        @pl.when(half == 1)
        def _():
            active = jnp.maximum(pre_act[slot, tick], 0)
            total[slot] += lax.dot_general(active, hbuf[tick, slot], TN, preferred_element_type=F32)

        @pl.when(jnp.logical_and(half == 1, tick == ticks - 1))
        def _():
            grad_out[slot] = total[slot].astype(BF16)

    def down_wait(slot):
        @pl.when(goes_down(slot))
        def _():
            wait_bytes(down_in.at[slot], down_recv.at[slot])

    def cross_scatter(slot):
        @pl.when(goes_down(slot))
        def _():
            term = lax.dot_general(w_up[slot], down_in[slot], (((0,), (1,)), ((), ())), preferred_element_type=F32)
            for half in range(2):
                part[first_g + slot * 2 + half] = term[half * rows:(half + 1) * rows].astype(BF16)
                scatter(first_g + slot * 2 + half)

    def cross_gather(slot):
        @pl.when(goes_down(slot))
        def _():
            for half in range(2):
                job = first_g + slot * 2 + half
                at = pl.ds(pl.multiple_of(half * rows + mine * piece, piece), piece)
                cross[slot, at, :] = gathered(job).astype(BF16)
                for rel in range(1, group):
                    send(cross.at[slot, at], cross.at[slot, at], g_send.at[slot * 2 + half],
                         g_recv.at[slot * 2 + half], peer(rel)[1]).start()

    def each(first, last, do):
        def body(step, carry):
            do(step)
            return carry

        lax.fori_loop(first, last, body, 0)

    def exchange_own(step):
        tick, slot, half, row = where_of(step)
        own_exchange(0, slot, half, step)

    def first_product(step):
        tick, slot, half, row = where_of(step)
        part[step] = lax.dot_general(
            hbuf[0, slot, pl.ds(row, rows), :], w_down[slot], NT, preferred_element_type=F32).astype(BF16)

    barrier = pltpu.get_barrier_semaphore()
    greeted = [peer(rel)[1] for rel in range(1, group)]
    greeted += [(sec, partner), (sec_below, ten), (sec_above, ten), (sec_below, partner), (sec_above, partner)]
    for other in greeted:
        pl.semaphore_signal(barrier, inc=1, device_id=other, device_id_type=MESH)

    loads = [pltpu.make_async_copy(src, dst, load_sem.at[i]) for i, (src, dst) in enumerate((
        (codes_hbm, codes), (down_hbm, w_down), (up_hbm, w_up), (pre_hbm, pre_act), (loss_hbm, loss_in)))]
    for load in loads[:4]:
        load.start()

    @pl.when(is_top)
    def _():
        loads[4].start()

    total[...] = jnp.zeros_like(total)
    loads[0].wait()
    lanes = min(128, rows)
    for slot in range(2):
        for block in range(tokens // lanes):
            at = slice(block * lanes, (block + 1) * lanes)
            across = jnp.broadcast_to(scales[slot:slot + 1, at], (lanes, lanes)).T
            for col in range(width // lanes):
                cols = slice(col * lanes, (col + 1) * lanes)
                hbuf[0, slot, at, cols] = (codes[slot, at, cols].astype(F32) * across).astype(BF16)
    loads[1].wait()
    each(0, CHAINS, first_product)
    loads[2].wait()
    loads[3].wait()
    each(0, CHAINS, add_weight_grad)
    pl.semaphore_wait(barrier, len(greeted))

    each(0, CHAINS, scatter)

    @pl.when(is_top)
    def _():
        loads[4].wait()
        for tick in range(1, ticks + 1):
            hbuf[tick, 1] = loss_in[entry[tick - 1]]

    def top_ahead(step, do):
        tick, slot, half, row = where_of(step)

        @pl.when(jnp.logical_and(enters(slot), tick + 1 < ticks))
        def _():
            do(tick + 1, slot, half, row, first_top + 2 * tick + half)

    def top_start(step):
        top_ahead(step, lambda tick, slot, half, row, job: own_partial(tick, slot, row, job))

    def top_exchange(step):
        top_ahead(step, lambda tick, slot, half, row, job: own_exchange(tick, slot, half, job))

    def look_first(step):
        tick, slot, half, row = where_of(step)

        @pl.when(goes_down(slot))
        def _():
            part[first_q + step] = lax.dot_general(
                passed[step], down_in[slot], NT, preferred_element_type=F32).astype(BF16)
            scatter(first_q + step)

    def pass_first(step):
        tick, slot, half, row = where_of(step)

        @pl.when(goes_down(slot))
        def _():
            gsum[first_q + step] = gathered(first_q + step).astype(BF16)
            send_sum(step)

    def take(step):
        tick, slot, half, row = where_of(step)
        arrive(tick, slot, half, row)
        look_ahead(step)
        top_start(step)

    each(0, CHAINS, exchange_own)

    @pl.when(is_top)
    def _():
        down_copy(0, 1).start()

    @pl.when(jnp.logical_not(is_top))
    def _():
        down_copy(1, 1).start()

    @pl.when(jnp.logical_not(is_top))
    def _():
        down_copy(0, 0).start()

    each(0, CHAINS, finish_hidden)

    each(0, CHAINS, update)
    down_wait(1)
    each(0, 2, look_first)
    each(0, 2, top_start)
    cross_scatter(1)
    each(0, 2, pass_first)
    each(0, 2, top_exchange)
    cross_gather(1)
    take(CHAINS)
    down_wait(0)
    each(2, CHAINS, look_first)
    cross_scatter(0)
    each(2, CHAINS, pass_first)
    cross_gather(0)

    def main(step):
        @pl.when(jnp.logical_and(step > CHAINS, step < steps))
        def _():
            take(step)

        @pl.when(step < steps)
        def _():
            finish_hidden(step)

        @pl.when(step > CHAINS)
        def _():
            pass_sum(step - 1)
            top_exchange(step - 1)
            update(step - 1)

        @pl.when(step < steps)
        def _():
            add_weight_grad(step)

    each(CHAINS, steps + 1, main)

    def hand_out(chain):
        tick, slot, half, row = where_of(chain)
        arrive(ticks, slot, half, row)
        held_out[slot, pl.ds(row, rows), :] = hbuf[ticks, slot, pl.ds(row, rows), :]

    each(0, CHAINS, hand_out)

    def drain(step):
        tick, slot, half, row = where_of(step)
        wait_bytes(rs_in.at[0], ag_send.at[step])

        @pl.when(goes_down(slot))
        def _():
            wait_bytes(passed.at[step], h_send.at[step])

        @pl.when(jnp.logical_and(step < jobs_q, goes_down(slot)))
        def _():
            wait_bytes(rs_in.at[0], rs_send.at[first_q + step])
            wait_bytes(msg.at[0, 0, 0], msg_send.at[first_q + step])

    def drain_own(job):
        wait_bytes(rs_in.at[0], rs_send.at[job])
        wait_bytes(gsum.at[0], msg_send.at[job])

    def drain_cross(job):
        @pl.when(goes_down(lax.div(job, 2)))
        def _():
            wait_bytes(rs_in.at[0], rs_send.at[first_g + job])
            wait_bytes(rs_in.at[0], g_send.at[job])

    each(0, steps, drain)
    each(0, CHAINS, drain_own)
    each(0, CHAINS, drain_cross)
    wait_bytes(w_down.at[0], down_send.at[0])

    @pl.when(is_top)
    def _():
        each(first_top, first_top + 2 * (ticks - 1), drain_own)

    @pl.when(jnp.logical_not(is_top))
    def _():
        wait_bytes(w_down.at[1], down_send.at[1])


def solution(mesh):
    sections, tensors = mesh.shape["section"], mesh.shape["tensor"]
    group = tensors // 2

    def per_device(grad_codes, token_scales, loss_grads, entry_order, w_up, w_down, pre_act):
        slots, tokens, width = grad_codes.shape
        ticks, hid = pre_act.shape[1], pre_act.shape[3]
        rows = tokens // 2
        piece = rows // group
        steps = ticks * CHAINS
        jobs = CHAINS * (ticks + 1) + 2 * (ticks - 1)
        vmem = pl.BlockSpec(memory_space=pltpu.VMEM)
        hbm = pl.BlockSpec(memory_space=pl.ANY)
        dma = pltpu.SemaphoreType.DMA
        return pl.pallas_call(
            lambda *refs: relay_kernel((sections, group, ticks, tokens, width), *refs),
            out_shape=(pltpu.VMEM((slots, tokens, width), BF16), pltpu.VMEM((slots, hid, width), BF16)),
            in_specs=[vmem, pl.BlockSpec(memory_space=pltpu.SMEM), hbm, hbm, hbm, hbm, hbm],
            out_specs=(vmem, vmem),
            scratch_shapes=[
                pltpu.VMEM((slots, tokens, width), jnp.int32),
                pltpu.VMEM((slots, width, hid), BF16),
                pltpu.VMEM((slots, hid, width), BF16),
                pltpu.VMEM((slots, ticks, tokens, hid), BF16),
                pltpu.VMEM((ticks, tokens, width), BF16),
                pltpu.VMEM((slots, hid, width), BF16),
                pltpu.VMEM((ticks + 1, slots, tokens, width), BF16),
                pltpu.VMEM((steps, rows, width), BF16),
                pltpu.VMEM((jobs, rows, hid), BF16),
                pltpu.VMEM((jobs, group - 1, piece, hid), BF16),
                pltpu.VMEM((jobs, piece, hid), BF16),
                pltpu.VMEM((ticks, slots, 2, 2, piece, hid), BF16),
                pltpu.VMEM((steps, rows, hid), BF16),
                pltpu.VMEM((slots, hid, hid), BF16),
                pltpu.VMEM((slots, hid, width), F32),
                dma((5,)), dma((jobs,)), dma((jobs,)), dma((jobs,)), dma((ticks, slots, 2)), dma((steps,)),
                dma((steps,)), dma((CHAINS,)), dma((CHAINS,)), dma((steps,)), dma((ticks, slots, 2)),
                dma((slots,)), dma((slots,)),
            ],
            compiler_params=pltpu.CompilerParams(
                collective_id=0, has_side_effects=True, vmem_limit_bytes=56 * 1024 * 1024),
            cost_estimate=pl.CostEstimate(flops=4 * 10**9, bytes_accessed=9 * 10**6, transcendentals=0),
        )(token_scales, entry_order, grad_codes, w_up, w_down, pre_act, loss_grads)

    placed = (
        P("section", None, "tensor"),
        P("section", None),
        P(None, None, "tensor"),
        P(),
        P("section", "tensor", None),
        P("section", None, "tensor"),
        P("section", None, None, None),
    )
    return jax.shard_map(
        per_device,
        mesh=mesh,
        in_specs=placed,
        out_specs=(P("section", None, "tensor"), P("section", None, "tensor")),
        check_vma=False,
    )
```

time: 146 us -> 133 us (0.911)
  Pallas kernels: 142 us -> 131 us
    pallas_call x1, Pallas kernels: 142 us -> 131 us  [per_device(): pl.pallas_call(lambda *refs: relay_kernel((sections, group, ticks, tokens...]
    unnamed x4 -> x2, local copies, waits for them, and re-layouts: 3.02 us -> 1.76 us
where the time goes in v3:
time: 133 us
  Pallas kernels  131 us (98%)
  local copies, waits for them, and re-layouts  1.76 us (1%)
    pallas_call x1, Pallas kernels, per_device(): pl.pallas_call(lambda *refs: relay_kernel((sections, group, ticks, tokens...  131 us

profile of v3, /device:TPU:1, one launch (start us, length us, event | category | flops | bytes accessed | tf_op | source)
XLA Modules:
  0.0 133.3 jit_solution(18352512447254242575)
XLA Ops:
  0.6 130.9 %shard_map.86 = (bf16[2,256,768]{2,1,0:T(8,128)(2,1)S(1)}, bf16[2,256,768]{2,1,0:T(8,128)(2,1)S(1)}) custom-call(f32[2,256]{1,0:T(2,128)} %refs_0_.1, s32[5]{0:T(128)} %refs_1_.1, s32[2,256,768]{2,1,0:T(8,128)} %refs_2_.1, bf16[2,768,256]{2,1,0:T(8,128)(2,1)} %refs_3_.1, bf16[2,256,768]{2,1,0:T(8,128)(2,1)} %refs_4_.1, bf16[2,5,256,256]{3,2,1,0:T(8,128)(2,1)} %refs_5_.1, ...), custom_call_target="tpu_custom_call" | custom-call | flops 4000000000 | bytes 9000000 | tf_op jit(solution)/shard_map/pallas_call | solution.py:392
  131.6 0.9 copy.11
  132.4 0.9 copy.12

commit v4 on v3

--- a/solution.py
+++ b/solution.py
@@ -204,8 +204,8 @@
             hbuf[0, slot, pl.ds(row, rows), :], w_down[slot], NT, preferred_element_type=F32).astype(BF16)
 
     barrier = pltpu.get_barrier_semaphore()
-    greeted = [peer(rel)[1] for rel in range(1, group)]
-    greeted += [(sec, partner), (sec_below, ten), (sec_above, ten), (sec_below, partner), (sec_above, partner)]
+    greeted = [(sec_below, partner), (sec_above, partner), (sec, partner), (sec_below, ten), (sec_above, ten)]
+    greeted += [peer(rel)[1] for rel in range(1, group)]
     for other in greeted:
         pl.semaphore_signal(barrier, inc=1, device_id=other, device_id_type=MESH)
 
@@ -289,24 +289,26 @@
     def _():
         down_copy(1, 1).start()
 
+    each(0, CHAINS, finish_hidden)
+
     @pl.when(jnp.logical_not(is_top))
     def _():
         down_copy(0, 0).start()
 
-    each(0, CHAINS, finish_hidden)
-
-    each(0, CHAINS, update)
+
+    each(0, 2, update)
     down_wait(1)
     each(0, 2, look_first)
     each(0, 2, top_start)
     cross_scatter(1)
     each(0, 2, pass_first)
     each(0, 2, top_exchange)
+    each(2, CHAINS, update)
     cross_gather(1)
-    take(CHAINS)
     down_wait(0)
     each(2, CHAINS, look_first)
     cross_scatter(0)
+    take(CHAINS)
     each(2, CHAINS, pass_first)
     cross_gather(0)
 
@@ -324,10 +326,7 @@
             pass_sum(step - 1)
             top_exchange(step - 1)
             update(step - 1)
-
-        @pl.when(step < steps)
-        def _():
-            add_weight_grad(step)
+            add_weight_grad(step - 1)
 
     each(CHAINS, steps + 1, main)
 

time: 133 us -> 133 us (level); the launches traced: 133 us -> 131 us
  Pallas kernels: 131 us -> 129 us
    pallas_call x1, Pallas kernels: 131 us -> 129 us  [per_device(): pl.pallas_call(lambda *refs: relay_kernel((sections, group, ticks, tokens...]
where the time goes in v4:
time: 133 us; the launch traced here: 131 us
  Pallas kernels  129 us (97%)
  local copies, waits for them, and re-layouts  1.76 us (1%)
    pallas_call x1, Pallas kernels, per_device(): pl.pallas_call(lambda *refs: relay_kernel((sections, group, ticks, tokens...  129 us

profile of v4, /device:TPU:1, one launch (start us, length us, event | category | flops | bytes accessed | tf_op | source)
XLA Modules:
  0.0 131.2 jit_solution(10107186991144206703)
XLA Ops:
  0.6 128.8 %shard_map.86 = (bf16[2,256,768]{2,1,0:T(8,128)(2,1)S(1)}, bf16[2,256,768]{2,1,0:T(8,128)(2,1)S(1)}) custom-call(f32[2,256]{1,0:T(2,128)} %refs_0_.1, s32[5]{0:T(128)} %refs_1_.1, s32[2,256,768]{2,1,0:T(8,128)} %refs_2_.1, bf16[2,768,256]{2,1,0:T(8,128)(2,1)} %refs_3_.1, bf16[2,256,768]{2,1,0:T(8,128)(2,1)} %refs_4_.1, bf16[2,5,256,256]{3,2,1,0:T(8,128)(2,1)} %refs_5_.1, ...), custom_call_target="tpu_custom_call" | custom-call | flops 4000000000 | bytes 9000000 | tf_op jit(solution)/shard_map/pallas_call | solution.py:391
  129.4 0.9 copy.11
  130.3 0.9 copy.12
